TPU v7x, 256 devices: a whole 4x4x8 slice. The times are simulated.
256 devices in a mesh: row: 16 (over y, x_lo, core), col: 16 (over z, x_hi).
Axes of the slice: x: 4 (x_hi: 2, x_lo: 2; x = x_hi * 2 + x_lo), y: 4, z: 8, core: 2. Of those that a mesh axis runs over, the one named last changes fastest.
Arguments:
- row_coefs: bfloat16 [14336, 16, 128], P('row', 'col'), may hold values from -8 to 8
- col_coefs: bfloat16 [14336, 16, 128], P('col', 'row'), may hold values from -8 to 8
- row_wedge: int32 [14336], P('row'), may hold values from 3 to 8
- col_wedge: int32 [14336], P('col'), may hold values from 3 to 8
- rotation: int32 [1], replicated, may hold values from 0 to 63
- best_in: float32 [14336, 14336], P('row', 'col'), may hold values from -0.3 to 0.5
Outputs:
- best_out: float32 [14336, 14336], P('row', 'col')
All inputs are finite; a program needn't handle non-finite values.
Results may differ from a plain program's by a relative error of at most 0.0015.
Values may be sent and summed in bfloat16 or wider, within the bound.
No kernel may reach another device: no remote copies, remote signals or barrier semaphores. Data moves between devices by JAX's collectives and lax.ppermute only.
A program may use at most 64 MiB of HBM per device.

v0:
```python
import functools

import jax
import jax.numpy as jnp
from jax import lax
from jax.experimental import pallas as pl
from jax.experimental.pallas import tpu as pltpu
from jax.sharding import PartitionSpec as P

BLOCK = 896
ANGLES = 64
HALF = 32
SHELLS = 16
NARROWEST = 3
LANES = 128
BAND = 2 * NARROWEST + 1
AXES = ("row", "col")


def coordinates():
    return [(y, xl, c, z, xh) for y in range(4) for xl in range(2) for c in range(2) for z in range(8) for xh in range(2)]


def flat(y, xl, c, z, xh):
    return (y * 4 + xl * 2 + c) * 16 + z * 2 + xh


def shift(x, dy=0, dxl=0, dc=0, dz=0, dxh=0):
    pairs = [
        (flat(y, xl, c, z, xh), flat((y + dy) % 4, (xl + dxl) % 2, (c + dc) % 2, (z + dz) % 8, (xh + dxh) % 2))
        for y, xl, c, z, xh in coordinates()
    ]
    return lax.ppermute(x, AXES, pairs)


def kept_bin(k, turn):
    first = NARROWEST + 1
    low = jnp.maximum(turn - NARROWEST, first)
    skipped = jnp.maximum(turn + NARROWEST + 1 - low, 0)
    place = k + first
    return jnp.where(place < low, place, place + skipped)


def wedge_mask(bins, turn, wedge):
    phase = (bins - turn) & (HALF - 1)
    return jnp.minimum(phase, HALF - phase) > wedge


def prepare_kernel(n, rotation_ref, row_ref, col_ref, row_wedge_ref, col_wedge_ref, row_out, col_out, rotation, row_coefs, col_coefs, row_wedge, col_wedge, sems):
    pairs = (
        (rotation_ref, rotation),
        (row_wedge_ref, row_wedge),
        (row_ref, row_coefs),
        (col_wedge_ref, col_wedge),
        (col_ref, col_coefs),
    )
    loads = [pltpu.make_async_copy(source, target, sems.at[i]) for i, (source, target) in enumerate(pairs)]
    for load in loads:
        load.start()
    loads[0].wait()
    offset = rotation[0] & (ANGLES - 1)
    turn = offset & (HALF - 1)
    rows = 4 * n

    def bins_of(shape):
        r = lax.broadcasted_iota(jnp.int32, shape, 0)
        part = jnp.where(r >= 2 * n, 1, 0)
        r = r - part * (2 * n)
        half = jnp.where(r >= n, 1, 0)
        return part, half, kept_bin(r - half * n, turn)

    part, half, bins = bins_of((rows, 2 * ANGLES))
    feature = lax.broadcasted_iota(jnp.int32, (rows, 2 * ANGLES), 1)
    angle = (bins + HALF * half + HALF // 2) & (ANGLES - 1)
    valid = bins < HALF - NARROWEST
    row_pick = jnp.where(valid & (feature == part * ANGLES + angle), 1.0, 0.0).astype(jnp.bfloat16)
    source = (angle - offset) & (ANGLES - 1)
    col_pick = jnp.where(valid & (feature == part * ANGLES + source), 1.0, 0.0).astype(jnp.bfloat16)
    _, _, bins = bins_of((rows, 1))
    for ready, pick, coefs, wedge, centre, out in (
        (loads[1:3], row_pick, row_coefs, row_wedge, 0, row_out),
        (loads[3:], col_pick, col_coefs, col_wedge, turn, col_out),
    ):
        for load in ready:
            load.wait()
        phase = (bins - centre) & (HALF - 1)
        spread = jnp.minimum(phase, HALF - phase)
        mask = spread > wedge[...].reshape(1, BLOCK)
        picked = lax.dot_general(pick, coefs[...], (((1,), (1,)), ((), ())), preferred_element_type=jnp.float32)
        out[0] = jnp.where(mask, picked, 0.0).astype(jnp.bfloat16)


def prepare(n, rotation, row_coefs, col_coefs, row_wedge, col_wedge):
    shape = jax.ShapeDtypeStruct((1, 4 * n, BLOCK), jnp.bfloat16)
    return pl.pallas_call(
        functools.partial(prepare_kernel, n),
        out_shape=[shape, shape],
        in_specs=[pl.BlockSpec(memory_space=pltpu.HBM)] * 5,
        out_specs=[pl.BlockSpec(memory_space=pltpu.VMEM)] * 2,
        scratch_shapes=[pltpu.SMEM((1,), jnp.int32)]
        + [pltpu.VMEM((BLOCK, 2 * ANGLES), jnp.bfloat16)] * 2
        + [pltpu.VMEM((BLOCK,), jnp.int32)] * 2
        + [pltpu.SemaphoreType.DMA((5,))],
        compiler_params=pltpu.CompilerParams(vmem_limit_bytes=8 * 1024 * 1024),
        name="prepare",
    )(rotation, row_coefs.reshape(BLOCK, 2 * ANGLES), col_coefs.reshape(BLOCK, 2 * ANGLES), row_wedge, col_wedge)


STRIPE = 448
FINISH_LIMIT = 16
STRIPES = BLOCK // STRIPE
SIDE = 64


def lanes(j):
    return pl.ds(pl.multiple_of(j * LANES, LANES), LANES)


def wedge_masks(n, rotation_ref, centre, wedge):
    turn = rotation_ref[0] & (HALF - 1)
    r = lax.broadcasted_iota(jnp.int32, (SIDE, LANES), 0)
    bins = kept_bin(r - jnp.where(r >= n, n, 0), turn)
    return jnp.where((r < 2 * n) & wedge_mask(bins, centre, wedge), 1.0, 0.0).astype(jnp.bfloat16)


def energy(n, total):
    both = (total[: 2 * n] + total[2 * n :]).astype(jnp.bfloat16)
    return jnp.concatenate([both, jnp.zeros((SIDE - 2 * n, LANES), jnp.bfloat16)])


def place(wide, slot, block, to):
    rows, deep = block.shape[0], wide.shape[1]
    wide[slot, pl.ds(0, rows), to] = block
    if deep > rows:
        wide[slot, pl.ds(rows, deep - rows), to] = jnp.zeros((deep - rows, LANES), jnp.bfloat16)


def product(a, b):
    return jnp.dot(a, b, preferred_element_type=jnp.float32)


def row_slot(dz, dxh):
    d = dz & 7
    return jnp.where(d == 0, 0, jnp.where(d <= 4, 2 * d - 1, 2 * (8 - d))) * 2 + dxh


def col_slot(dy, dxl, dc):
    me_row, me_col = lax.axis_index("row"), lax.axis_index("col")
    y, xl, c = me_row >> 2, (me_row >> 1) & 1, me_row & 1
    z, xh = me_col >> 1, me_col & 1
    shell = ((y - dy) & 3) * 4 + (xl ^ dxl) * 2 + (c ^ dc)
    return row_slot(z - (shell >> 1), xh ^ (shell & 1))


def gathered(pieces, total, wide, slots, at, to):
    shells = [piece[i, :, at] for piece in pieces for i in range(piece.shape[0])]
    for slot, block in zip(slots, shells):
        place(wide, slot, block, to)
        squares = jnp.square(block.astype(jnp.float32))
        total = squares if total is None else total + squares
    return total


def turned_rows(left, column, at, start):
    wide = column.shape[0] * column.shape[1]
    left[at, pl.ds(start, wide)] = column[...].reshape(wide, LANES).T


def begin_kernel(places, *refs):
    rows, chip = refs[:4], refs[4]
    left, right, row_sums, col_sums, column = refs[5:]
    slots = [col_slot(dy, dxl, 0) for dy, dxl in places]

    def assemble(j, carry):
        at = lanes(j)
        row_sums[:, at] = gathered(rows, None, column, range(8), at, pl.ds(0, LANES))
        turned_rows(left, column, at, 0)
        col_sums[:, at] = gathered([chip], None, right, slots, at, at)
        return carry

    lax.fori_loop(0, BLOCK // LANES, assemble, 0)


def partial_kernel(n, places, rotation_ref, col_wedge_ref, down2, up3, down3, other, early_row_sums, early_col_sums, _, __, left, right, cross_ref, sums_ref, col_masks, col_energies, column):
    deep = right.shape[1]
    start = 8 * deep
    slots = [col_slot(dy, dxl, 1) for dy, dxl in places]
    turn = rotation_ref[0] & (HALF - 1)
    nothing = jnp.zeros((SIDE, LANES), jnp.bfloat16)

    def assemble(j, carry):
        at = lanes(j)
        sums_ref[:, at] = gathered([down2, up3, down3], early_row_sums[:, at], column, range(6), at, pl.ds(0, LANES))
        turned_rows(left, column, at, start)
        total = gathered([other], early_col_sums[:, at], right, slots, at, at)
        col_masks[:, at] = jnp.concatenate([wedge_masks(n, rotation_ref, turn, col_wedge_ref[:, at]), nothing])
        col_energies[:, at] = jnp.concatenate([nothing, energy(n, total)])
        return carry

    lax.fori_loop(0, BLOCK // LANES, assemble, 0)

    def stripe(m, carry):
        at = pl.ds(pl.multiple_of(m * STRIPE, STRIPE), STRIPE)
        cross_ref[at, :] = product(left[at, :], right[: SHELLS - 2].reshape((SHELLS - 2) * deep, BLOCK))
        return carry

    lax.fori_loop(0, STRIPES, stripe, 0, unroll=True)


def finish_kernel(n, rotation_ref, row_wedge_ref, best_ref, cross_ref, sums_ref, right, col_masks, col_energies, first, second, out_ref, column, left, side):
    late = left.shape[1]

    def assemble(j, carry):
        at = lanes(j)
        total = gathered([first, second], sums_ref[:, at], column, range(2), at, pl.ds(0, LANES))
        turned_rows(left, column, at, 0)
        side[at, :] = jnp.concatenate([energy(n, total), wedge_masks(n, rotation_ref, 0, row_wedge_ref[:, at])]).T
        return carry

    lax.fori_loop(0, BLOCK // LANES, assemble, 0)

    def stripe(m, carry):
        at = pl.ds(pl.multiple_of(m * STRIPE, STRIPE), STRIPE)
        cross = cross_ref[at, :] + product(left[at, :], right[SHELLS - 2 :].reshape(late, BLOCK))
        row_norm = product(side[at, :], col_masks[...])
        col_norm = product(side[at, :], col_energies[...])
        score = cross * lax.rsqrt(row_norm * col_norm + 1e-06)
        out_ref[at, :] = jnp.maximum(best_ref[at, :], score)
        return carry

    lax.fori_loop(0, STRIPES, stripe, 0, unroll=True)


SMEM, VMEM = pl.BlockSpec(memory_space=pltpu.SMEM), pl.BlockSpec(memory_space=pltpu.VMEM)
MIB = 1024 * 1024


def begin(n, rows, chip, places):
    deep = -(-4 * n // 16) * 16
    sums = jax.ShapeDtypeStruct((4 * n, BLOCK), jnp.float32)
    return pl.pallas_call(
        functools.partial(begin_kernel, places),
        out_shape=[
            jax.ShapeDtypeStruct((BLOCK, (SHELLS - 2) * deep), jnp.bfloat16),
            jax.ShapeDtypeStruct((SHELLS, deep, BLOCK), jnp.bfloat16),
            sums,
            sums,
        ],
        in_specs=[VMEM] * 5,
        out_specs=[VMEM] * 4,
        scratch_shapes=[pltpu.VMEM((8, deep, LANES), jnp.bfloat16)],
        compiler_params=pltpu.CompilerParams(vmem_limit_bytes=8 * MIB),
        cost_estimate=pl.CostEstimate(flops=16 * 8 * n * BLOCK, bytes_accessed=6 * MIB, transcendentals=0),
        name="begin",
    )(*rows, chip)


def partial_cross(n, rotation, col_wedge, late, other, begun, places):
    left, right, row_sums, col_sums = begun
    deep = right.shape[1]
    sides = jax.ShapeDtypeStruct((2 * SIDE, BLOCK), jnp.bfloat16)
    return pl.pallas_call(
        functools.partial(partial_kernel, n, places),
        out_shape=[
            jax.ShapeDtypeStruct(left.shape, left.dtype),
            jax.ShapeDtypeStruct(right.shape, right.dtype),
            jax.ShapeDtypeStruct((BLOCK, BLOCK), jnp.float32),
            jax.ShapeDtypeStruct((4 * n, BLOCK), jnp.float32),
            sides,
            sides,
        ],
        in_specs=[SMEM] + [VMEM] * 9,
        out_specs=[VMEM] * 6,
        scratch_shapes=[pltpu.VMEM((6, deep, LANES), jnp.bfloat16)],
        input_output_aliases={8: 0, 9: 1},
        compiler_params=pltpu.CompilerParams(vmem_limit_bytes=16 * MIB),
        cost_estimate=pl.CostEstimate(flops=2 * BLOCK * BLOCK * (SHELLS - 2) * deep, bytes_accessed=8 * MIB, transcendentals=0),
        name="partial_cross",
    )(rotation, col_wedge, *late, other, row_sums, col_sums, left, right)


def finish(n, rotation, row_wedge, best_in, cross, sums, right, col_masks, col_energies, last):
    deep = right.shape[1]
    return pl.pallas_call(
        functools.partial(finish_kernel, n),
        out_shape=jax.ShapeDtypeStruct((BLOCK, BLOCK), jnp.float32),
        in_specs=[SMEM] + [VMEM] * 9,
        out_specs=VMEM,
        scratch_shapes=[
            pltpu.VMEM((2, deep, LANES), jnp.bfloat16),
            pltpu.VMEM((BLOCK, 2 * deep), jnp.bfloat16),
            pltpu.VMEM((BLOCK, LANES), jnp.bfloat16),
        ],
        compiler_params=pltpu.CompilerParams(vmem_limit_bytes=FINISH_LIMIT * MIB),
        cost_estimate=pl.CostEstimate(flops=2 * BLOCK * BLOCK * (2 * deep + 4 * SIDE), bytes_accessed=8 * MIB, transcendentals=BLOCK * BLOCK),
        name="finish",
    )(rotation, row_wedge, best_in, cross, sums, right, col_masks, col_energies, *last)


def with_bins(n, row_coefs, col_coefs, row_wedge, col_wedge, rotation, best_in):
    row_own, col_own = prepare(n, rotation, row_coefs, col_coefs, row_wedge, col_wedge)
    row_wedge, col_wedge = row_wedge.reshape(1, BLOCK), col_wedge.reshape(1, BLOCK)
    together = lax.optimization_barrier
    pair = jnp.concatenate([row_own, shift(row_own, dxh=1)])
    pair, col_own = together((pair, col_own))
    up1, down1 = shift(pair, dz=1), shift(pair, dz=-1)
    col_pair = jnp.concatenate([col_own, shift(col_own, dxl=1)])
    up1, down1, col_pair = together((up1, down1, col_pair))
    up2, down2 = shift(up1, dz=1), shift(down1, dz=-1)
    north, south, across = shift(col_pair, dy=1), shift(col_pair, dy=-1), shift(col_pair, dy=2)
    places = [(dy, dxl) for dy in (0, 1, -1, 2) for dxl in (0, 1)]
    up2, down2 = together((up2, down2))
    chip = jnp.concatenate([col_pair, north, south, across])
    up3, down3 = shift(up2, dz=1), shift(down2, dz=-1)
    begun = begin(n, (pair, up1, down1, up2), chip, places)
    up3, down3, chip, begun = together((up3, down3, chip, begun))
    other = shift(chip, dc=1)
    last = (shift(up3[:1], dz=1), shift(down3[1:], dz=-1))
    _, right, cross, sums, masks, energies = partial_cross(n, rotation, col_wedge, (down2, up3, down3), other, begun, places)
    return finish(n, rotation, row_wedge, best_in, cross, sums, right, masks, energies, last)


def shards(row_coefs, col_coefs, row_wedge, col_wedge, rotation, best_in):
    turn = rotation[0] & (HALF - 1)
    apart = jnp.minimum(jnp.minimum(turn, HALF - turn), BAND)
    branches = [functools.partial(with_bins, n) for n in (18, 20, 22, 24, 26)]
    return lax.cond(apart < BAND, functools.partial(with_bins, 26), functools.partial(with_bins, 18), row_coefs, col_coefs, row_wedge, col_wedge, rotation, best_in)


def solution(mesh):
    return jax.shard_map(
        shards,
        mesh=mesh,
        in_specs=(
            P("row", "col", None),
            P("col", "row", None),
            P("row"),
            P("col"),
            P(),
            P("row", "col"),
        ),
        out_specs=P("row", "col"),
        check_vma=False,
    )
```

profile of v0, /device:TPU:1, one launch (start us, length us, event | category | flops | bytes accessed | tf_op | source)
XLA Modules:
  0.0 53.3 jit_solution(8466326996884863103)
XLA Ops:
  0.7 51.0 %conditional.1 = (f32[896,896]{1,0:T(8,128)S(1)}) conditional(s32[]{:T(128)} %convert_element_type.3, (s32[896]{0:T(1024)}, s32[896]{0:T(1024)}, bf16[896,1,128]{2,0,1:T(8,128)(2,1)}, bf16[896,1,128]{2,0,1:T(8,128)(2,1)}, s32[1]{0:T(128)}, /*index=5*/f32[896,896]{1,0:T(8,128)}) %tuple.19, (s32[896]{0:T(1024)}, s32[896]{0:T(1024)}, ...), branch_computations={%region_0.0_spmd, %region_1.0_spmd} | conditional | flops 3291688960 | bytes 63539852 | solution.py:327
  0.7 2.1 %prepare.2 = (bf16[1,72,896]{2,1,0:T(8,128)(2,1)S(1)}, bf16[1,72,896]{2,1,0:T(8,128)(2,1)S(1)}) custom-call(s32[1]{0:T(128)} %get-tuple-element.32.rotation_ref, bf16[896,128]{1,0:T(8,128)(2,1)} %bitcast.5, bf16[896,128]{1,0:T(8,128)(2,1)} %bitcast.7, s32[896]{0:T(1024)} %get-tuple-element.33.row_wedge_ref, s32[896]{0:T(1024)} %get-tuple-element.35.col_wedge_ref), custom_call_target="tpu_custom_call" | custom-call | tf_op jit(solution)/shard_map/cond/branch_0_fun/prepare/pallas_call | solution.py:95
  2.7 3.7 %collective-permute-start = (bf16[1,72,896]{2,1,0:T(8,128)(2,1)S(1)}, bf16[1,72,896]{2,1,0:T(8,128)(2,1)S(1)}, u32[]{:S(2)}, u32[]{:S(2)}) collective-permute-start(bf16[1,72,896]{2,1,0:T(8,128)(2,1)S(1)} %get-tuple-element.38), channel_id=1, source_target_pairs={{0,1},{1,0},{2,3},{3,2},{4,5},{5,4},{6,7},{7,6},{8,9},{9,8},{10,11... | collective-permute-start | bytes 387080 | tf_op jit(solution)/shard_map/cond/branch_0_fun/ppermute | solution.py:33
  6.4 2.3 %collective-permute-done = bf16[1,72,896]{2,1,0:T(8,128)(2,1)S(1)} collective-permute-done((bf16[1,72,896]{2,1,0:T(8,128)(2,1)S(1)}, bf16[1,72,896]{2,1,0:T(8,128)(2,1)S(1)}, u32[]{:S(2)}, u32[]{:S(2)}) %collective-permute-start) | collective-permute-done | bytes 129056 | tf_op jit(solution)/shard_map/cond/branch_0_fun/ppermute | solution.py:33
  8.8 2.5 %collective-permute-start.1 = (bf16[2,72,896]{2,1,0:T(8,128)(2,1)S(1)}, bf16[2,72,896]{2,1,0:T(8,128)(2,1)S(1)}, u32[]{:S(2)}, u32[]{:S(2)}) collective-permute-start(bf16[2,72,896]{2,1,0:T(8,128)(2,1)S(1)} %pad_maximum_fusion.refs_0_), channel_id=1, source_target_pairs={{0,2},{1,3},{2,4},{3,5},{4,6},{5,7},{6,8},{7,9},{8,10},{9,11},{10,... | collective-permute-start | bytes 774152 | tf_op jit(solution)/shard_map/cond/branch_0_fun/ppermute | solution.py:33
  11.2 4.0 %collective-permute-start.2 = (bf16[2,72,896]{2,1,0:T(8,128)(2,1)S(1)}, bf16[2,72,896]{2,1,0:T(8,128)(2,1)S(1)}, u32[]{:S(2)}, u32[]{:S(2)}) collective-permute-start(bf16[2,72,896]{2,1,0:T(8,128)(2,1)S(1)} %pad_maximum_fusion.refs_0_), channel_id=1, source_target_pairs={{0,14},{1,15},{2,0},{3,1},{4,2},{5,3},{6,4},{7,5},{8,6},{9,7},{10,... | collective-permute-start | bytes 774152 | tf_op jit(solution)/shard_map/cond/branch_0_fun/ppermute | solution.py:33
  15.3 1.2 %collective-permute-start.3 = (bf16[1,72,896]{2,1,0:T(8,128)(2,1)S(1)}, bf16[1,72,896]{2,1,0:T(8,128)(2,1)S(1)}, u32[]{:S(2)}, u32[]{:S(2)}) collective-permute-start(bf16[1,72,896]{2,1,0:T(8,128)(2,1)S(1)} %get-tuple-element.41), channel_id=1, source_target_pairs={{0,32},{1,33},{2,34},{3,35},{4,36},{5,37},{6,38},{7,39},{8,40},{9,... | collective-permute-start | bytes 387080 | tf_op jit(solution)/shard_map/cond/branch_0_fun/ppermute | solution.py:33
  16.5 2.9 %collective-permute-done.3 = bf16[1,72,896]{2,1,0:T(8,128)(2,1)S(1)} collective-permute-done((bf16[1,72,896]{2,1,0:T(8,128)(2,1)S(1)}, bf16[1,72,896]{2,1,0:T(8,128)(2,1)S(1)}, u32[]{:S(2)}, u32[]{:S(2)}) %collective-permute-start.3) | collective-permute-done | bytes 129056 | tf_op jit(solution)/shard_map/cond/branch_0_fun/ppermute | solution.py:33
  19.4 0.0 copy-start.5
  19.4 0.0 copy-start.3
  19.4 0.7 %collective-permute-done.1.refs_1_ = bf16[2,72,896]{2,1,0:T(8,128)(2,1)S(1)} collective-permute-done((bf16[2,72,896]{2,1,0:T(8,128)(2,1)S(1)}, bf16[2,72,896]{2,1,0:T(8,128)(2,1)S(1)}, u32[]{:S(2)}, u32[]{:S(2)}) %collective-permute-start.1) | collective-permute-done | bytes 258080 | tf_op jit(solution)/shard_map/cond/branch_0_fun/ppermute | solution.py:33
  20.2 0.0 collective-permute-done.2.refs_2_
  20.2 0.0 collective-permute-start.4
  20.2 2.7 %collective-permute-start.5 = (bf16[2,72,896]{2,1,0:T(8,128)(2,1)S(1)}, bf16[2,72,896]{2,1,0:T(8,128)(2,1)S(1)}, u32[]{:S(2)}, u32[]{:S(2)}) collective-permute-start(bf16[2,72,896]{2,1,0:T(8,128)(2,1)S(1)} %collective-permute-done.2.refs_2_), channel_id=1, source_target_pairs={{0,14},{1,15},{2,0},{3,1},{4,2},{5,3},{6,4},{7,5},{8,6},{9,7},{10,... | collective-permute-start | bytes 774152 | tf_op jit(solution)/shard_map/cond/branch_0_fun/ppermute | solution.py:33
  22.8 1.3 %collective-permute-start.8 = (bf16[2,72,896]{2,1,0:T(8,128)(2,1)S(1)}, bf16[2,72,896]{2,1,0:T(8,128)(2,1)S(1)}, u32[]{:S(2)}, u32[]{:S(2)}) collective-permute-start(bf16[2,72,896]{2,1,0:T(8,128)(2,1)S(1)} %pad_maximum_fusion.1), channel_id=1, source_target_pairs={{0,64},{1,65},{2,66},{3,67},{4,68},{5,69},{6,70},{7,71},{8,72},{9,... | collective-permute-start | bytes 774152 | tf_op jit(solution)/shard_map/cond/branch_0_fun/ppermute | solution.py:33
  24.1 1.4 %collective-permute-start.9 = (bf16[2,72,896]{2,1,0:T(8,128)(2,1)S(1)}, bf16[2,72,896]{2,1,0:T(8,128)(2,1)S(1)}, u32[]{:S(2)}, u32[]{:S(2)}) collective-permute-start(bf16[2,72,896]{2,1,0:T(8,128)(2,1)S(1)} %pad_maximum_fusion.1), channel_id=1, source_target_pairs={{0,192},{1,193},{2,194},{3,195},{4,196},{5,197},{6,198},{7,199},{8... | collective-permute-start | bytes 774152 | tf_op jit(solution)/shard_map/cond/branch_0_fun/ppermute | solution.py:33
  25.6 1.6 %collective-permute-start.10 = (bf16[2,72,896]{2,1,0:T(8,128)(2,1)S(1)}, bf16[2,72,896]{2,1,0:T(8,128)(2,1)S(1)}, u32[]{:S(2)}, u32[]{:S(2)}) collective-permute-start(bf16[2,72,896]{2,1,0:T(8,128)(2,1)S(1)} %pad_maximum_fusion.1), channel_id=1, source_target_pairs={{0,128},{1,129},{2,130},{3,131},{4,132},{5,133},{6,134},{7,135},{8... | collective-permute-start | bytes 774152 | tf_op jit(solution)/shard_map/cond/branch_0_fun/ppermute | solution.py:33
  27.3 0.0 collective-permute-done.4.refs_3_
  27.3 0.0 collective-permute-done.5.down2
  27.3 1.1 %collective-permute-start.6 = (bf16[2,72,896]{2,1,0:T(8,128)(2,1)S(1)}, bf16[2,72,896]{2,1,0:T(8,128)(2,1)S(1)}, u32[]{:S(2)}, u32[]{:S(2)}) collective-permute-start(bf16[2,72,896]{2,1,0:T(8,128)(2,1)S(1)} %collective-permute-done.4.refs_3_), channel_id=1, source_target_pairs={{0,2},{1,3},{2,4},{3,5},{4,6},{5,7},{6,8},{7,9},{8,10},{9,11},{10,... | collective-permute-start | bytes 774152 | tf_op jit(solution)/shard_map/cond/branch_0_fun/ppermute | solution.py:33
  28.4 1.6 %collective-permute-start.7 = (bf16[2,72,896]{2,1,0:T(8,128)(2,1)S(1)}, bf16[2,72,896]{2,1,0:T(8,128)(2,1)S(1)}, u32[]{:S(2)}, u32[]{:S(2)}) collective-permute-start(bf16[2,72,896]{2,1,0:T(8,128)(2,1)S(1)} %collective-permute-done.5.down2), channel_id=1, source_target_pairs={{0,14},{1,15},{2,0},{3,1},{4,2},{5,3},{6,4},{7,5},{8,6},{9,7},{10,... | collective-permute-start | bytes 774152 | tf_op jit(solution)/shard_map/cond/branch_0_fun/ppermute | solution.py:33
  30.0 0.0 collective-permute-done.8
  30.1 0.0 collective-permute-done.9
  30.1 5.4 %collective-permute-done.10 = bf16[2,72,896]{2,1,0:T(8,128)(2,1)S(1)} collective-permute-done((bf16[2,72,896]{2,1,0:T(8,128)(2,1)S(1)}, bf16[2,72,896]{2,1,0:T(8,128)(2,1)S(1)}, u32[]{:S(2)}, u32[]{:S(2)}) %collective-permute-start.10) | collective-permute-done | bytes 258080 | tf_op jit(solution)/shard_map/cond/branch_0_fun/ppermute | solution.py:33
  35.5 1.0 %begin.2 = (bf16[896,1120]{1,0:T(8,128)(2,1)S(1)}, bf16[16,80,896]{2,1,0:T(8,128)(2,1)S(1)}, f32[72,896]{1,0:T(8,128)S(1)}, f32[72,896]{1,0:T(8,128)S(1)}) custom-call(bf16[2,72,896]{2,1,0:T(8,128)(2,1)S(1)} %pad_maximum_fusion.refs_0_, bf16[2,72,896]{2,1,0:T(8,128)(2,1)S(1)} %collective-permute-done.1.refs_1_, ...), custom_call_target="tpu_custom_call" | custom-call | flops 2064384 | bytes 6291456 | tf_op jit(solution)/shard_map/cond/branch_0_fun/begin/pallas_call | solution.py:241
  36.5 0.0 collective-permute-done.6.up3
  36.5 0.0 collective-permute-done.7.down3
  36.6 4.1 %collective-permute-start.11 = (bf16[8,72,896]{2,1,0:T(8,128)(2,1)S(1)}, bf16[8,72,896]{2,1,0:T(8,128)(2,1)S(1)}, u32[]{:S(2)}, u32[]{:S(2)}) collective-permute-start(bf16[8,72,896]{2,1,0:T(8,128)(2,1)S(1)} %constant_dynamic-update-slice_fusion.refs_4_), channel_id=1, source_target_pairs={{0,16},{1,17},{2,18},{3,19},{4,20},{5,21},{6,22},{7,23},{8,24},{9,... | collective-permute-start | bytes 3096584 | tf_op jit(solution)/shard_map/cond/branch_0_fun/ppermute | solution.py:33
  40.6 0.0 copy-done.5
  40.6 0.0 copy-done.3
  40.6 0.1 collective-permute-start.12
  40.8 0.0 copy-start
  40.8 2.9 %collective-permute-start.13 = (bf16[1,72,896]{2,1,0:T(8,128)(2,1)S(1)}, bf16[1,72,896]{2,1,0:T(8,128)(2,1)S(1)}, u32[]{:S(2)}, u32[]{:S(2)}) collective-permute-start(bf16[1,72,896]{2,1,0:T(8,128)(2,1)S(1)} %slice.9), channel_id=1, source_target_pairs={{0,14},{1,15},{2,0},{3,1},{4,2},{5,3},{6,4},{7,5},{8,6},{9,7},{10,... | collective-permute-start | bytes 387080 | tf_op jit(solution)/shard_map/cond/branch_0_fun/ppermute | solution.py:33
  43.7 0.0 collective-permute-done.11.other
  43.7 4.2 %partial_cross.2 = (bf16[896,1120]{1,0:T(8,128)(2,1)S(1)}, bf16[16,80,896]{2,1,0:T(8,128)(2,1)S(1)}, f32[896,896]{1,0:T(8,128)S(1)}, f32[72,896]{1,0:T(8,128)S(1...) custom-call(s32[1]{0:T(128)} %get-tuple-element.32.rotation_ref, ...), custom_call_target="tpu_custom_call", output_to_operand_aliasing={{0}: (8, {}), {1}: (9, {})} | custom-call | flops 1798307840 | bytes 8388608 | tf_op jit(solution)/shard_map/cond/branch_0_fun/partial_cross/pallas_call | solution.py:262
  47.9 0.0 collective-permute-done.12.first
  47.9 0.0 collective-permute-done.13.second
  47.9 0.0 copy-done
  47.9 3.2 %finish.2 = f32[896,896]{1,0:T(8,128)S(1)} custom-call(s32[1]{0:T(128)} %get-tuple-element.32.rotation_ref, s32[1,896]{1,0:T(1,128)S(1)} %reshape.18.row_wedge_ref, f32[896,896]{1,0:T(8,128)S(1)} %copy-done, f32[896,896]{1,0:T(8,128)S(1)} %get-tuple-element.58.cross_ref, f32[72,896]{1,0:T(8,128)S(1)} %get-tuple-element.59.sums_ref, ...), custom_call_target="tpu_custom_call" | custom-call | flops 667942912 | bytes 8388608 | tf_op jit(solution)/shard_map/cond/branch_0_fun/finish/pallas_call | solution.py:284
  51.6 0.0 copy-start.2
  51.6 1.7 %copy-done.2 = f32[896,896]{1,0:T(8,128)} copy-done((f32[896,896]{1,0:T(8,128)}, f32[896,896]{1,0:T(8,128)S(1)}, u32[]{:S(2)}) %copy-start.2) | copy-done | bytes 3211288
  (10 shorter events, 0.2 us)
Async XLA Ops:
  2.7 6.0 %collective-permute-start = (bf16[1,72,896]{2,1,0:T(8,128)(2,1)S(1)}, bf16[1,72,896]{2,1,0:T(8,128)(2,1)S(1)}, u32[]{:S(2)}, u32[]{:S(2)}) collective-permute-start(bf16[1,72,896]{2,1,0:T(8,128)(2,1)S(1)} %get-tuple-element.38), channel_id=1, source_target_pairs={{0,1},{1,0},{2,3},{3,2},{4,5},{5,4},{6,7},{7,6},{8,9},{9,8},{10,11... | collective-permute-start | bytes 387080 | tf_op jit(solution)/shard_map/cond/branch_0_fun/ppermute | solution.py:33
  8.8 11.4 %collective-permute-start.1 = (bf16[2,72,896]{2,1,0:T(8,128)(2,1)S(1)}, bf16[2,72,896]{2,1,0:T(8,128)(2,1)S(1)}, u32[]{:S(2)}, u32[]{:S(2)}) collective-permute-start(bf16[2,72,896]{2,1,0:T(8,128)(2,1)S(1)} %pad_maximum_fusion.refs_0_), channel_id=1, source_target_pairs={{0,2},{1,3},{2,4},{3,5},{4,6},{5,7},{6,8},{7,9},{8,10},{9,11},{10,... | collective-permute-start | bytes 774152 | tf_op jit(solution)/shard_map/cond/branch_0_fun/ppermute | solution.py:33
  11.2 8.9 %collective-permute-start.2 = (bf16[2,72,896]{2,1,0:T(8,128)(2,1)S(1)}, bf16[2,72,896]{2,1,0:T(8,128)(2,1)S(1)}, u32[]{:S(2)}, u32[]{:S(2)}) collective-permute-start(bf16[2,72,896]{2,1,0:T(8,128)(2,1)S(1)} %pad_maximum_fusion.refs_0_), channel_id=1, source_target_pairs={{0,14},{1,15},{2,0},{3,1},{4,2},{5,3},{6,4},{7,5},{8,6},{9,7},{10,... | collective-permute-start | bytes 774152 | tf_op jit(solution)/shard_map/cond/branch_0_fun/ppermute | solution.py:33
  15.3 4.1 %collective-permute-start.3 = (bf16[1,72,896]{2,1,0:T(8,128)(2,1)S(1)}, bf16[1,72,896]{2,1,0:T(8,128)(2,1)S(1)}, u32[]{:S(2)}, u32[]{:S(2)}) collective-permute-start(bf16[1,72,896]{2,1,0:T(8,128)(2,1)S(1)} %get-tuple-element.41), channel_id=1, source_target_pairs={{0,32},{1,33},{2,34},{3,35},{4,36},{5,37},{6,38},{7,39},{8,40},{9,... | collective-permute-start | bytes 387080 | tf_op jit(solution)/shard_map/cond/branch_0_fun/ppermute | solution.py:33
  19.4 21.2 %copy-start.5 = (s32[896]{0:T(1024)S(1)}, s32[896]{0:T(1024)}, u32[]{:S(2)}) copy-start(s32[896]{0:T(1024)} %get-tuple-element.35.col_wedge_ref) | copy-start | bytes 10756 | tf_op jit(solution)/shard_map/cond
  19.4 21.2 %copy-start.3 = (s32[896]{0:T(1024)S(1)}, s32[896]{0:T(1024)}, u32[]{:S(2)}) copy-start(s32[896]{0:T(1024)} %get-tuple-element.33.row_wedge_ref) | copy-start | bytes 10756 | tf_op jit(solution)/shard_map/cond
  20.2 7.1 %collective-permute-start.4 = (bf16[2,72,896]{2,1,0:T(8,128)(2,1)S(1)}, bf16[2,72,896]{2,1,0:T(8,128)(2,1)S(1)}, u32[]{:S(2)}, u32[]{:S(2)}) collective-permute-start(bf16[2,72,896]{2,1,0:T(8,128)(2,1)S(1)} %collective-permute-done.1.refs_1_), channel_id=1, source_target_pairs={{0,2},{1,3},{2,4},{3,5},{4,6},{5,7},{6,8},{7,9},{8,10},{9,11},{10,... | collective-permute-start | bytes 774152 | tf_op jit(solution)/shard_map/cond/branch_0_fun/ppermute | solution.py:33
  20.2 7.1 %collective-permute-start.5 = (bf16[2,72,896]{2,1,0:T(8,128)(2,1)S(1)}, bf16[2,72,896]{2,1,0:T(8,128)(2,1)S(1)}, u32[]{:S(2)}, u32[]{:S(2)}) collective-permute-start(bf16[2,72,896]{2,1,0:T(8,128)(2,1)S(1)} %collective-permute-done.2.refs_2_), channel_id=1, source_target_pairs={{0,14},{1,15},{2,0},{3,1},{4,2},{5,3},{6,4},{7,5},{8,6},{9,7},{10,... | collective-permute-start | bytes 774152 | tf_op jit(solution)/shard_map/cond/branch_0_fun/ppermute | solution.py:33
  22.8 7.2 %collective-permute-start.8 = (bf16[2,72,896]{2,1,0:T(8,128)(2,1)S(1)}, bf16[2,72,896]{2,1,0:T(8,128)(2,1)S(1)}, u32[]{:S(2)}, u32[]{:S(2)}) collective-permute-start(bf16[2,72,896]{2,1,0:T(8,128)(2,1)S(1)} %pad_maximum_fusion.1), channel_id=1, source_target_pairs={{0,64},{1,65},{2,66},{3,67},{4,68},{5,69},{6,70},{7,71},{8,72},{9,... | collective-permute-start | bytes 774152 | tf_op jit(solution)/shard_map/cond/branch_0_fun/ppermute | solution.py:33
  24.1 5.9 %collective-permute-start.9 = (bf16[2,72,896]{2,1,0:T(8,128)(2,1)S(1)}, bf16[2,72,896]{2,1,0:T(8,128)(2,1)S(1)}, u32[]{:S(2)}, u32[]{:S(2)}) collective-permute-start(bf16[2,72,896]{2,1,0:T(8,128)(2,1)S(1)} %pad_maximum_fusion.1), channel_id=1, source_target_pairs={{0,192},{1,193},{2,194},{3,195},{4,196},{5,197},{6,198},{7,199},{8... | collective-permute-start | bytes 774152 | tf_op jit(solution)/shard_map/cond/branch_0_fun/ppermute | solution.py:33
  25.6 9.9 %collective-permute-start.10 = (bf16[2,72,896]{2,1,0:T(8,128)(2,1)S(1)}, bf16[2,72,896]{2,1,0:T(8,128)(2,1)S(1)}, u32[]{:S(2)}, u32[]{:S(2)}) collective-permute-start(bf16[2,72,896]{2,1,0:T(8,128)(2,1)S(1)} %pad_maximum_fusion.1), channel_id=1, source_target_pairs={{0,128},{1,129},{2,130},{3,131},{4,132},{5,133},{6,134},{7,135},{8... | collective-permute-start | bytes 774152 | tf_op jit(solution)/shard_map/cond/branch_0_fun/ppermute | solution.py:33
  27.3 9.3 %collective-permute-start.6 = (bf16[2,72,896]{2,1,0:T(8,128)(2,1)S(1)}, bf16[2,72,896]{2,1,0:T(8,128)(2,1)S(1)}, u32[]{:S(2)}, u32[]{:S(2)}) collective-permute-start(bf16[2,72,896]{2,1,0:T(8,128)(2,1)S(1)} %collective-permute-done.4.refs_3_), channel_id=1, source_target_pairs={{0,2},{1,3},{2,4},{3,5},{4,6},{5,7},{6,8},{7,9},{8,10},{9,11},{10,... | collective-permute-start | bytes 774152 | tf_op jit(solution)/shard_map/cond/branch_0_fun/ppermute | solution.py:33
  28.4 8.1 %collective-permute-start.7 = (bf16[2,72,896]{2,1,0:T(8,128)(2,1)S(1)}, bf16[2,72,896]{2,1,0:T(8,128)(2,1)S(1)}, u32[]{:S(2)}, u32[]{:S(2)}) collective-permute-start(bf16[2,72,896]{2,1,0:T(8,128)(2,1)S(1)} %collective-permute-done.5.down2), channel_id=1, source_target_pairs={{0,14},{1,15},{2,0},{3,1},{4,2},{5,3},{6,4},{7,5},{8,6},{9,7},{10,... | collective-permute-start | bytes 774152 | tf_op jit(solution)/shard_map/cond/branch_0_fun/ppermute | solution.py:33
  36.6 7.1 %collective-permute-start.11 = (bf16[8,72,896]{2,1,0:T(8,128)(2,1)S(1)}, bf16[8,72,896]{2,1,0:T(8,128)(2,1)S(1)}, u32[]{:S(2)}, u32[]{:S(2)}) collective-permute-start(bf16[8,72,896]{2,1,0:T(8,128)(2,1)S(1)} %constant_dynamic-update-slice_fusion.refs_4_), channel_id=1, source_target_pairs={{0,16},{1,17},{2,18},{3,19},{4,20},{5,21},{6,22},{7,23},{8,24},{9,... | collective-permute-start | bytes 3096584 | tf_op jit(solution)/shard_map/cond/branch_0_fun/ppermute | solution.py:33
  40.6 7.2 %collective-permute-start.12 = (bf16[1,72,896]{2,1,0:T(8,128)(2,1)S(1)}, bf16[1,72,896]{2,1,0:T(8,128)(2,1)S(1)}, u32[]{:S(2)}, u32[]{:S(2)}) collective-permute-start(bf16[1,72,896]{2,1,0:T(8,128)(2,1)S(1)} %slice.8), channel_id=1, source_target_pairs={{0,2},{1,3},{2,4},{3,5},{4,6},{5,7},{6,8},{7,9},{8,10},{9,11},{10,... | collective-permute-start | bytes 387080 | tf_op jit(solution)/shard_map/cond/branch_0_fun/ppermute | solution.py:33
  40.8 7.2 %copy-start = (f32[896,896]{1,0:T(8,128)S(1)}, f32[896,896]{1,0:T(8,128)}, u32[]{:S(2)}) copy-start(f32[896,896]{1,0:T(8,128)} %get-tuple-element.34.best_ref) | copy-start | bytes 9633796 | tf_op jit(solution)/shard_map/cond
  40.8 7.1 %collective-permute-start.13 = (bf16[1,72,896]{2,1,0:T(8,128)(2,1)S(1)}, bf16[1,72,896]{2,1,0:T(8,128)(2,1)S(1)}, u32[]{:S(2)}, u32[]{:S(2)}) collective-permute-start(bf16[1,72,896]{2,1,0:T(8,128)(2,1)S(1)} %slice.9), channel_id=1, source_target_pairs={{0,14},{1,15},{2,0},{3,1},{4,2},{5,3},{6,4},{7,5},{8,6},{9,7},{10,... | collective-permute-start | bytes 387080 | tf_op jit(solution)/shard_map/cond/branch_0_fun/ppermute | solution.py:33
  51.6 1.7 %copy-start.2 = (f32[896,896]{1,0:T(8,128)}, f32[896,896]{1,0:T(8,128)S(1)}, u32[]{:S(2)}) copy-start(f32[896,896]{1,0:T(8,128)S(1)} %get-tuple-element.133) | copy-start | bytes 9633796
where the time goes:
time: 53.4 us; the launch traced here: 53.3 us
  starting transfers between devices  28.2 us (53%)
  waiting for transfers between devices  11.4 us (21%)
  Pallas kernels  10.4 us (19%)
  local copies, waits for them, and re-layouts  1.84 us (3%)
  loops' own time  0.72 us (1%)
  between operations  0.67 us (1%)
    ppermute x14, starting transfers between devices, shift(): return lax.ppermute(x, AXES, pairs)  28.2 us
    ppermute x14, waiting for transfers between devices, shift(): return lax.ppermute(x, AXES, pairs)  11.4 us
    pallas_call x1, Pallas kernels, partial_cross(): pl.pallas_call(functools.partial(partial_kernel, n, places), out_shape=[j...  4.2 us
    pallas_call x1, Pallas kernels, finish(): pl.pallas_call(functools.partial(finish_kernel, n), out_shape=jax.ShapeDt...  3.16 us
    pallas_call x1, Pallas kernels, prepare(): pl.pallas_call(functools.partial(prepare_kernel, n), out_shape=[shape, sh...  2.07 us
    unnamed x2, local copies, waits for them, and re-layouts  1.68 us
  transfers between devices with their start and end apart: 14, of which 4 were waited for; matrix products, arithmetic and copies ran while one was open for 0% of the time, Pallas kernels for 10%

commit v1 on v0

--- a/solution.py
+++ b/solution.py
@@ -167,24 +167,24 @@
 
 
 def begin_kernel(places, *refs):
-    rows, chip = refs[:4], refs[4]
-    left, right, row_sums, col_sums, column = refs[5:]
-    slots = [col_slot(dy, dxl, 0) for dy, dxl in places]
+    rows, cols = refs[:4], refs[4:7]
+    left, right, row_sums, col_sums, column = refs[7:]
+    slots = [col_slot(dy, dxl, 0) for dy, dxl in places[:6]]
 
     def assemble(j, carry):
         at = lanes(j)
         row_sums[:, at] = gathered(rows, None, column, range(8), at, pl.ds(0, LANES))
         turned_rows(left, column, at, 0)
-        col_sums[:, at] = gathered([chip], None, right, slots, at, at)
+        col_sums[:, at] = gathered(cols, None, right, slots, at, at)
         return carry
 
     lax.fori_loop(0, BLOCK // LANES, assemble, 0)
 
 
-def partial_kernel(n, places, rotation_ref, col_wedge_ref, down2, up3, down3, other, early_row_sums, early_col_sums, _, __, left, right, cross_ref, sums_ref, col_masks, col_energies, column):
+def partial_kernel(n, places, rotation_ref, col_wedge_ref, down2, up3, down3, across, other, early_row_sums, early_col_sums, _, __, left, right, cross_ref, sums_ref, col_masks, col_energies, column):
     deep = right.shape[1]
     start = 8 * deep
-    slots = [col_slot(dy, dxl, 1) for dy, dxl in places]
+    slots = [col_slot(dy, dxl, 0) for dy, dxl in places[6:]] + [col_slot(dy, dxl, 1) for dy, dxl in places]
     turn = rotation_ref[0] & (HALF - 1)
     nothing = jnp.zeros((SIDE, LANES), jnp.bfloat16)
 
@@ -192,7 +192,7 @@
         at = lanes(j)
         sums_ref[:, at] = gathered([down2, up3, down3], early_row_sums[:, at], column, range(6), at, pl.ds(0, LANES))
         turned_rows(left, column, at, start)
-        total = gathered([other], early_col_sums[:, at], right, slots, at, at)
+        total = gathered([across, other], early_col_sums[:, at], right, slots, at, at)
         col_masks[:, at] = jnp.concatenate([wedge_masks(n, rotation_ref, turn, col_wedge_ref[:, at]), nothing])
         col_energies[:, at] = jnp.concatenate([nothing, energy(n, total)])
         return carry
@@ -235,7 +235,7 @@
 MIB = 1024 * 1024
 
 
-def begin(n, rows, chip, places):
+def begin(n, rows, cols, places):
     deep = -(-4 * n // 16) * 16
     sums = jax.ShapeDtypeStruct((4 * n, BLOCK), jnp.float32)
     return pl.pallas_call(
@@ -246,16 +246,16 @@
             sums,
             sums,
         ],
-        in_specs=[VMEM] * 5,
+        in_specs=[VMEM] * 7,
         out_specs=[VMEM] * 4,
         scratch_shapes=[pltpu.VMEM((8, deep, LANES), jnp.bfloat16)],
         compiler_params=pltpu.CompilerParams(vmem_limit_bytes=8 * MIB),
         cost_estimate=pl.CostEstimate(flops=16 * 8 * n * BLOCK, bytes_accessed=6 * MIB, transcendentals=0),
         name="begin",
-    )(*rows, chip)
-
-
-def partial_cross(n, rotation, col_wedge, late, other, begun, places):
+    )(*rows, *cols)
+
+
+def partial_cross(n, rotation, col_wedge, late, across, other, begun, places):
     left, right, row_sums, col_sums = begun
     deep = right.shape[1]
     sides = jax.ShapeDtypeStruct((2 * SIDE, BLOCK), jnp.bfloat16)
@@ -269,14 +269,14 @@
             sides,
             sides,
         ],
-        in_specs=[SMEM] + [VMEM] * 9,
+        in_specs=[SMEM] + [VMEM] * 10,
         out_specs=[VMEM] * 6,
         scratch_shapes=[pltpu.VMEM((6, deep, LANES), jnp.bfloat16)],
-        input_output_aliases={8: 0, 9: 1},
+        input_output_aliases={9: 0, 10: 1},
         compiler_params=pltpu.CompilerParams(vmem_limit_bytes=16 * MIB),
         cost_estimate=pl.CostEstimate(flops=2 * BLOCK * BLOCK * (SHELLS - 2) * deep, bytes_accessed=8 * MIB, transcendentals=0),
         name="partial_cross",
-    )(rotation, col_wedge, *late, other, row_sums, col_sums, left, right)
+    )(rotation, col_wedge, *late, across, other, row_sums, col_sums, left, right)
 
 
 def finish(n, rotation, row_wedge, best_in, cross, sums, right, col_masks, col_energies, last):
@@ -312,11 +312,11 @@
     up2, down2 = together((up2, down2))
     chip = jnp.concatenate([col_pair, north, south, across])
     up3, down3 = shift(up2, dz=1), shift(down2, dz=-1)
-    begun = begin(n, (pair, up1, down1, up2), chip, places)
+    begun = begin(n, (pair, up1, down1, up2), (col_pair, north, south), places)
     up3, down3, chip, begun = together((up3, down3, chip, begun))
     other = shift(chip, dc=1)
     last = (shift(up3[:1], dz=1), shift(down3[1:], dz=-1))
-    _, right, cross, sums, masks, energies = partial_cross(n, rotation, col_wedge, (down2, up3, down3), other, begun, places)
+    _, right, cross, sums, masks, energies = partial_cross(n, rotation, col_wedge, (down2, up3, down3), across, other, begun, places)
     return finish(n, rotation, row_wedge, best_in, cross, sums, right, masks, energies, last)
 
 

time: 53.4 us -> 52.8 us (0.989)
  waiting for transfers between devices: 11.4 us -> 10.7 us
    ppermute x14, waiting for transfers between devices: 11.4 us -> 10.7 us  [shift(): return lax.ppermute(x, AXES, pairs)]
where the time goes in v1:
time: 52.8 us; the launch traced here: 52.7 us
  starting transfers between devices  28.2 us (53%)
  waiting for transfers between devices  10.7 us (20%)
  Pallas kernels  10.5 us (20%)
  local copies, waits for them, and re-layouts  1.73 us (3%)
  loops' own time  0.67 us (1%)
  between operations  0.67 us (1%)
    ppermute x14, starting transfers between devices, shift(): return lax.ppermute(x, AXES, pairs)  28.2 us
    ppermute x14, waiting for transfers between devices, shift(): return lax.ppermute(x, AXES, pairs)  10.7 us
    pallas_call x1, Pallas kernels, partial_cross(): pl.pallas_call(functools.partial(partial_kernel, n, places), out_shape=[j...  4.27 us
    pallas_call x1, Pallas kernels, finish(): pl.pallas_call(functools.partial(finish_kernel, n), out_shape=jax.ShapeDt...  3.29 us
    pallas_call x1, Pallas kernels, prepare(): pl.pallas_call(functools.partial(prepare_kernel, n), out_shape=[shape, sh...  2.07 us
    unnamed x2, local copies, waits for them, and re-layouts  1.68 us
  transfers between devices with their start and end apart: 14, of which 4 were waited for; matrix products, arithmetic and copies ran while one was open for 0% of the time, Pallas kernels for 10%

profile of v1, /device:TPU:1, one launch (start us, length us, event | category | flops | bytes accessed | tf_op | source)
XLA Modules:
  0.0 52.7 jit_solution(13300689482426572774)
XLA Ops:
  0.7 50.3 %conditional.1 = (f32[896,896]{1,0:T(8,128)S(1)}) conditional(s32[]{:T(128)} %convert_element_type.3, (s32[896]{0:T(1024)}, s32[896]{0:T(1024)}, bf16[896,1,128]{2,0,1:T(8,128)(2,1)}, bf16[896,1,128]{2,0,1:T(8,128)(2,1)}, s32[1]{0:T(128)}, /*index=5*/f32[896,896]{1,0:T(8,128)}) %tuple.19, (s32[896]{0:T(1024)}, s32[896]{0:T(1024)}, ...), branch_computations={%region_0.0_spmd, %region_1.0_spmd} | conditional | flops 3293925376 | bytes 63539852 | solution.py:327
  0.7 2.1 %prepare.2 = (bf16[1,72,896]{2,1,0:T(8,128)(2,1)S(1)}, bf16[1,72,896]{2,1,0:T(8,128)(2,1)S(1)}) custom-call(s32[1]{0:T(128)} %get-tuple-element.32.rotation_ref, bf16[896,128]{1,0:T(8,128)(2,1)} %bitcast.5, bf16[896,128]{1,0:T(8,128)(2,1)} %bitcast.7, s32[896]{0:T(1024)} %get-tuple-element.33.row_wedge_ref, s32[896]{0:T(1024)} %get-tuple-element.35.col_wedge_ref), custom_call_target="tpu_custom_call" | custom-call | tf_op jit(solution)/shard_map/cond/branch_0_fun/prepare/pallas_call | solution.py:95
  2.7 3.7 %collective-permute-start = (bf16[1,72,896]{2,1,0:T(8,128)(2,1)S(1)}, bf16[1,72,896]{2,1,0:T(8,128)(2,1)S(1)}, u32[]{:S(2)}, u32[]{:S(2)}) collective-permute-start(bf16[1,72,896]{2,1,0:T(8,128)(2,1)S(1)} %get-tuple-element.38), channel_id=1, source_target_pairs={{0,1},{1,0},{2,3},{3,2},{4,5},{5,4},{6,7},{7,6},{8,9},{9,8},{10,11... | collective-permute-start | bytes 387080 | tf_op jit(solution)/shard_map/cond/branch_0_fun/ppermute | solution.py:33
  6.4 2.3 %collective-permute-done = bf16[1,72,896]{2,1,0:T(8,128)(2,1)S(1)} collective-permute-done((bf16[1,72,896]{2,1,0:T(8,128)(2,1)S(1)}, bf16[1,72,896]{2,1,0:T(8,128)(2,1)S(1)}, u32[]{:S(2)}, u32[]{:S(2)}) %collective-permute-start) | collective-permute-done | bytes 129056 | tf_op jit(solution)/shard_map/cond/branch_0_fun/ppermute | solution.py:33
  8.8 0.0 copy-start.5
  8.8 0.0 copy-start.3
  8.8 2.5 %collective-permute-start.1 = (bf16[2,72,896]{2,1,0:T(8,128)(2,1)S(1)}, bf16[2,72,896]{2,1,0:T(8,128)(2,1)S(1)}, u32[]{:S(2)}, u32[]{:S(2)}) collective-permute-start(bf16[2,72,896]{2,1,0:T(8,128)(2,1)S(1)} %pad_maximum_fusion.1.refs_0_), channel_id=1, source_target_pairs={{0,2},{1,3},{2,4},{3,5},{4,6},{5,7},{6,8},{7,9},{8,10},{9,11},{10,... | collective-permute-start | bytes 774152 | tf_op jit(solution)/shard_map/cond/branch_0_fun/ppermute | solution.py:33
  11.3 4.0 %collective-permute-start.2 = (bf16[2,72,896]{2,1,0:T(8,128)(2,1)S(1)}, bf16[2,72,896]{2,1,0:T(8,128)(2,1)S(1)}, u32[]{:S(2)}, u32[]{:S(2)}) collective-permute-start(bf16[2,72,896]{2,1,0:T(8,128)(2,1)S(1)} %pad_maximum_fusion.1.refs_0_), channel_id=1, source_target_pairs={{0,14},{1,15},{2,0},{3,1},{4,2},{5,3},{6,4},{7,5},{8,6},{9,7},{10,... | collective-permute-start | bytes 774152 | tf_op jit(solution)/shard_map/cond/branch_0_fun/ppermute | solution.py:33
  15.3 1.2 %collective-permute-start.3 = (bf16[1,72,896]{2,1,0:T(8,128)(2,1)S(1)}, bf16[1,72,896]{2,1,0:T(8,128)(2,1)S(1)}, u32[]{:S(2)}, u32[]{:S(2)}) collective-permute-start(bf16[1,72,896]{2,1,0:T(8,128)(2,1)S(1)} %get-tuple-element.41), channel_id=1, source_target_pairs={{0,32},{1,33},{2,34},{3,35},{4,36},{5,37},{6,38},{7,39},{8,40},{9,... | collective-permute-start | bytes 387080 | tf_op jit(solution)/shard_map/cond/branch_0_fun/ppermute | solution.py:33
  16.5 2.9 %collective-permute-done.3 = bf16[1,72,896]{2,1,0:T(8,128)(2,1)S(1)} collective-permute-done((bf16[1,72,896]{2,1,0:T(8,128)(2,1)S(1)}, bf16[1,72,896]{2,1,0:T(8,128)(2,1)S(1)}, u32[]{:S(2)}, u32[]{:S(2)}) %collective-permute-start.3) | collective-permute-done | bytes 129056 | tf_op jit(solution)/shard_map/cond/branch_0_fun/ppermute | solution.py:33
  19.4 0.8 %collective-permute-done.1.refs_1_ = bf16[2,72,896]{2,1,0:T(8,128)(2,1)S(1)} collective-permute-done((bf16[2,72,896]{2,1,0:T(8,128)(2,1)S(1)}, bf16[2,72,896]{2,1,0:T(8,128)(2,1)S(1)}, u32[]{:S(2)}, u32[]{:S(2)}) %collective-permute-start.1) | collective-permute-done | bytes 258080 | tf_op jit(solution)/shard_map/cond/branch_0_fun/ppermute | solution.py:33
  20.2 0.0 collective-permute-done.2.refs_2_
  20.2 0.0 collective-permute-start.4
  20.2 2.7 %collective-permute-start.5 = (bf16[2,72,896]{2,1,0:T(8,128)(2,1)S(1)}, bf16[2,72,896]{2,1,0:T(8,128)(2,1)S(1)}, u32[]{:S(2)}, u32[]{:S(2)}) collective-permute-start(bf16[2,72,896]{2,1,0:T(8,128)(2,1)S(1)} %collective-permute-done.2.refs_2_), channel_id=1, source_target_pairs={{0,14},{1,15},{2,0},{3,1},{4,2},{5,3},{6,4},{7,5},{8,6},{9,7},{10,... | collective-permute-start | bytes 774152 | tf_op jit(solution)/shard_map/cond/branch_0_fun/ppermute | solution.py:33
  22.9 1.3 %collective-permute-start.8 = (bf16[2,72,896]{2,1,0:T(8,128)(2,1)S(1)}, bf16[2,72,896]{2,1,0:T(8,128)(2,1)S(1)}, u32[]{:S(2)}, u32[]{:S(2)}) collective-permute-start(bf16[2,72,896]{2,1,0:T(8,128)(2,1)S(1)} %pad_maximum_fusion.2.refs_4_), channel_id=1, source_target_pairs={{0,64},{1,65},{2,66},{3,67},{4,68},{5,69},{6,70},{7,71},{8,72},{9,... | collective-permute-start | bytes 774152 | tf_op jit(solution)/shard_map/cond/branch_0_fun/ppermute | solution.py:33
  24.2 1.4 %collective-permute-start.9 = (bf16[2,72,896]{2,1,0:T(8,128)(2,1)S(1)}, bf16[2,72,896]{2,1,0:T(8,128)(2,1)S(1)}, u32[]{:S(2)}, u32[]{:S(2)}) collective-permute-start(bf16[2,72,896]{2,1,0:T(8,128)(2,1)S(1)} %pad_maximum_fusion.2.refs_4_), channel_id=1, source_target_pairs={{0,192},{1,193},{2,194},{3,195},{4,196},{5,197},{6,198},{7,199},{8... | collective-permute-start | bytes 774152 | tf_op jit(solution)/shard_map/cond/branch_0_fun/ppermute | solution.py:33
  25.6 1.6 %collective-permute-start.10 = (bf16[2,72,896]{2,1,0:T(8,128)(2,1)S(1)}, bf16[2,72,896]{2,1,0:T(8,128)(2,1)S(1)}, u32[]{:S(2)}, u32[]{:S(2)}) collective-permute-start(bf16[2,72,896]{2,1,0:T(8,128)(2,1)S(1)} %pad_maximum_fusion.2.refs_4_), channel_id=1, source_target_pairs={{0,128},{1,129},{2,130},{3,131},{4,132},{5,133},{6,134},{7,135},{8... | collective-permute-start | bytes 774152 | tf_op jit(solution)/shard_map/cond/branch_0_fun/ppermute | solution.py:33
  27.3 0.0 collective-permute-done.4.refs_3_
  27.3 0.0 collective-permute-done.5.down2
  27.3 1.2 %collective-permute-start.6 = (bf16[2,72,896]{2,1,0:T(8,128)(2,1)S(1)}, bf16[2,72,896]{2,1,0:T(8,128)(2,1)S(1)}, u32[]{:S(2)}, u32[]{:S(2)}) collective-permute-start(bf16[2,72,896]{2,1,0:T(8,128)(2,1)S(1)} %collective-permute-done.4.refs_3_), channel_id=1, source_target_pairs={{0,2},{1,3},{2,4},{3,5},{4,6},{5,7},{6,8},{7,9},{8,10},{9,11},{10,... | collective-permute-start | bytes 774152 | tf_op jit(solution)/shard_map/cond/branch_0_fun/ppermute | solution.py:33
  28.4 1.5 %collective-permute-start.7 = (bf16[2,72,896]{2,1,0:T(8,128)(2,1)S(1)}, bf16[2,72,896]{2,1,0:T(8,128)(2,1)S(1)}, u32[]{:S(2)}, u32[]{:S(2)}) collective-permute-start(bf16[2,72,896]{2,1,0:T(8,128)(2,1)S(1)} %collective-permute-done.5.down2), channel_id=1, source_target_pairs={{0,14},{1,15},{2,0},{3,1},{4,2},{5,3},{6,4},{7,5},{8,6},{9,7},{10,... | collective-permute-start | bytes 774152 | tf_op jit(solution)/shard_map/cond/branch_0_fun/ppermute | solution.py:33
  29.9 0.0 collective-permute-done.8.refs_5_
  29.9 0.0 collective-permute-done.9.refs_6_
  29.9 0.9 %begin.2 = (bf16[896,1120]{1,0:T(8,128)(2,1)S(1)}, bf16[16,80,896]{2,1,0:T(8,128)(2,1)S(1)}, f32[72,896]{1,0:T(8,128)S(1)}, f32[72,896]{1,0:T(8,128)S(1)}) custom-call(bf16[2,72,896]{2,1,0:T(8,128)(2,1)S(1)} %pad_maximum_fusion.1.refs_0_, bf16[2,72,896]{2,1,0:T(8,128)(2,1)S(1)} %collective-permute-done.1.refs_1_, ...), custom_call_target="tpu_custom_call" | custom-call | flops 2064384 | bytes 6291456 | tf_op jit(solution)/shard_map/cond/branch_0_fun/begin/pallas_call | solution.py:241
  30.8 4.7 %collective-permute-done.10.across = bf16[2,72,896]{2,1,0:T(8,128)(2,1)S(1)} collective-permute-done((bf16[2,72,896]{2,1,0:T(8,128)(2,1)S(1)}, bf16[2,72,896]{2,1,0:T(8,128)(2,1)S(1)}, u32[]{:S(2)}, u32[]{:S(2)}) %collective-permute-start.10) | collective-permute-done | bytes 258080 | tf_op jit(solution)/shard_map/cond/branch_0_fun/ppermute | solution.py:33
  35.5 0.2 pad_maximum_fusion
  35.7 0.0 collective-permute-done.6.up3
  35.7 0.0 collective-permute-done.7.down3
  35.7 4.1 %collective-permute-start.11 = (bf16[8,72,896]{2,1,0:T(8,128)(2,1)S(1)}, bf16[8,72,896]{2,1,0:T(8,128)(2,1)S(1)}, u32[]{:S(2)}, u32[]{:S(2)}) collective-permute-start(bf16[8,72,896]{2,1,0:T(8,128)(2,1)S(1)} %pad_maximum_fusion), channel_id=1, source_target_pairs={{0,16},{1,17},{2,18},{3,19},{4,20},{5,21},{6,22},{7,23},{8,24},{9,... | collective-permute-start | bytes 3096584 | tf_op jit(solution)/shard_map/cond/branch_0_fun/ppermute | solution.py:33
  39.8 0.0 copy-done.5
  39.8 0.0 copy-done.3
  39.8 0.8 %collective-permute-start.12 = (bf16[1,72,896]{2,1,0:T(8,128)(2,1)S(1)}, bf16[1,72,896]{2,1,0:T(8,128)(2,1)S(1)}, u32[]{:S(2)}, u32[]{:S(2)}) collective-permute-start(bf16[1,72,896]{2,1,0:T(8,128)(2,1)S(1)} %slice.8), channel_id=1, source_target_pairs={{0,2},{1,3},{2,4},{3,5},{4,6},{5,7},{6,8},{7,9},{8,10},{9,11},{10,... | collective-permute-start | bytes 387080 | tf_op jit(solution)/shard_map/cond/branch_0_fun/ppermute | solution.py:33
  40.6 0.0 copy-start
  40.6 2.2 %collective-permute-start.13 = (bf16[1,72,896]{2,1,0:T(8,128)(2,1)S(1)}, bf16[1,72,896]{2,1,0:T(8,128)(2,1)S(1)}, u32[]{:S(2)}, u32[]{:S(2)}) collective-permute-start(bf16[1,72,896]{2,1,0:T(8,128)(2,1)S(1)} %slice.9), channel_id=1, source_target_pairs={{0,14},{1,15},{2,0},{3,1},{4,2},{5,3},{6,4},{7,5},{8,6},{9,7},{10,... | collective-permute-start | bytes 387080 | tf_op jit(solution)/shard_map/cond/branch_0_fun/ppermute | solution.py:33
  42.8 0.0 collective-permute-done.11.other
  42.8 4.3 %partial_cross.2 = (bf16[896,1120]{1,0:T(8,128)(2,1)S(1)}, bf16[16,80,896]{2,1,0:T(8,128)(2,1)S(1)}, f32[896,896]{1,0:T(8,128)S(1)}, f32[72,896]{1,0:T(8,128)S(1...) custom-call(s32[1]{0:T(128)} %get-tuple-element.32.rotation_ref, ...), custom_call_target="tpu_custom_call", output_to_operand_aliasing={{0}: (9, {}), {1}: (10, {})} | custom-call | flops 1798307840 | bytes 8388608 | tf_op jit(solution)/shard_map/cond/branch_0_fun/partial_cross/pallas_call | solution.py:262
  47.1 0.0 collective-permute-done.12.first
  47.1 0.0 collective-permute-done.13.second
  47.1 0.0 copy-done
  47.1 3.3 %finish.2 = f32[896,896]{1,0:T(8,128)S(1)} custom-call(s32[1]{0:T(128)} %get-tuple-element.32.rotation_ref, s32[1,896]{1,0:T(1,128)S(1)} %reshape.18.row_wedge_ref, f32[896,896]{1,0:T(8,128)S(1)} %copy-done, f32[896,896]{1,0:T(8,128)S(1)} %get-tuple-element.58.cross_ref, f32[72,896]{1,0:T(8,128)S(1)} %get-tuple-element.59.sums_ref, ...), custom_call_target="tpu_custom_call" | custom-call | flops 667942912 | bytes 8388608 | tf_op jit(solution)/shard_map/cond/branch_0_fun/finish/pallas_call | solution.py:284
  51.0 0.0 copy-start.2
  51.0 1.7 %copy-done.2 = f32[896,896]{1,0:T(8,128)} copy-done((f32[896,896]{1,0:T(8,128)}, f32[896,896]{1,0:T(8,128)S(1)}, u32[]{:S(2)}) %copy-start.2) | copy-done | bytes 3211288
  (6 shorter events, 0.1 us)
Async XLA Ops:
  2.7 6.0 %collective-permute-start = (bf16[1,72,896]{2,1,0:T(8,128)(2,1)S(1)}, bf16[1,72,896]{2,1,0:T(8,128)(2,1)S(1)}, u32[]{:S(2)}, u32[]{:S(2)}) collective-permute-start(bf16[1,72,896]{2,1,0:T(8,128)(2,1)S(1)} %get-tuple-element.38), channel_id=1, source_target_pairs={{0,1},{1,0},{2,3},{3,2},{4,5},{5,4},{6,7},{7,6},{8,9},{9,8},{10,11... | collective-permute-start | bytes 387080 | tf_op jit(solution)/shard_map/cond/branch_0_fun/ppermute | solution.py:33
  8.8 31.0 %copy-start.5 = (s32[896]{0:T(1024)S(1)}, s32[896]{0:T(1024)}, u32[]{:S(2)}) copy-start(s32[896]{0:T(1024)} %get-tuple-element.35.col_wedge_ref) | copy-start | bytes 10756 | tf_op jit(solution)/shard_map/cond
  8.8 31.0 %copy-start.3 = (s32[896]{0:T(1024)S(1)}, s32[896]{0:T(1024)}, u32[]{:S(2)}) copy-start(s32[896]{0:T(1024)} %get-tuple-element.33.row_wedge_ref) | copy-start | bytes 10756 | tf_op jit(solution)/shard_map/cond
  8.8 11.4 %collective-permute-start.1 = (bf16[2,72,896]{2,1,0:T(8,128)(2,1)S(1)}, bf16[2,72,896]{2,1,0:T(8,128)(2,1)S(1)}, u32[]{:S(2)}, u32[]{:S(2)}) collective-permute-start(bf16[2,72,896]{2,1,0:T(8,128)(2,1)S(1)} %pad_maximum_fusion.1.refs_0_), channel_id=1, source_target_pairs={{0,2},{1,3},{2,4},{3,5},{4,6},{5,7},{6,8},{7,9},{8,10},{9,11},{10,... | collective-permute-start | bytes 774152 | tf_op jit(solution)/shard_map/cond/branch_0_fun/ppermute | solution.py:33
  11.3 8.9 %collective-permute-start.2 = (bf16[2,72,896]{2,1,0:T(8,128)(2,1)S(1)}, bf16[2,72,896]{2,1,0:T(8,128)(2,1)S(1)}, u32[]{:S(2)}, u32[]{:S(2)}) collective-permute-start(bf16[2,72,896]{2,1,0:T(8,128)(2,1)S(1)} %pad_maximum_fusion.1.refs_0_), channel_id=1, source_target_pairs={{0,14},{1,15},{2,0},{3,1},{4,2},{5,3},{6,4},{7,5},{8,6},{9,7},{10,... | collective-permute-start | bytes 774152 | tf_op jit(solution)/shard_map/cond/branch_0_fun/ppermute | solution.py:33
  15.3 4.1 %collective-permute-start.3 = (bf16[1,72,896]{2,1,0:T(8,128)(2,1)S(1)}, bf16[1,72,896]{2,1,0:T(8,128)(2,1)S(1)}, u32[]{:S(2)}, u32[]{:S(2)}) collective-permute-start(bf16[1,72,896]{2,1,0:T(8,128)(2,1)S(1)} %get-tuple-element.41), channel_id=1, source_target_pairs={{0,32},{1,33},{2,34},{3,35},{4,36},{5,37},{6,38},{7,39},{8,40},{9,... | collective-permute-start | bytes 387080 | tf_op jit(solution)/shard_map/cond/branch_0_fun/ppermute | solution.py:33
  20.2 7.1 %collective-permute-start.4 = (bf16[2,72,896]{2,1,0:T(8,128)(2,1)S(1)}, bf16[2,72,896]{2,1,0:T(8,128)(2,1)S(1)}, u32[]{:S(2)}, u32[]{:S(2)}) collective-permute-start(bf16[2,72,896]{2,1,0:T(8,128)(2,1)S(1)} %collective-permute-done.1.refs_1_), channel_id=1, source_target_pairs={{0,2},{1,3},{2,4},{3,5},{4,6},{5,7},{6,8},{7,9},{8,10},{9,11},{10,... | collective-permute-start | bytes 774152 | tf_op jit(solution)/shard_map/cond/branch_0_fun/ppermute | solution.py:33
  20.2 7.1 %collective-permute-start.5 = (bf16[2,72,896]{2,1,0:T(8,128)(2,1)S(1)}, bf16[2,72,896]{2,1,0:T(8,128)(2,1)S(1)}, u32[]{:S(2)}, u32[]{:S(2)}) collective-permute-start(bf16[2,72,896]{2,1,0:T(8,128)(2,1)S(1)} %collective-permute-done.2.refs_2_), channel_id=1, source_target_pairs={{0,14},{1,15},{2,0},{3,1},{4,2},{5,3},{6,4},{7,5},{8,6},{9,7},{10,... | collective-permute-start | bytes 774152 | tf_op jit(solution)/shard_map/cond/branch_0_fun/ppermute | solution.py:33
  22.9 7.1 %collective-permute-start.8 = (bf16[2,72,896]{2,1,0:T(8,128)(2,1)S(1)}, bf16[2,72,896]{2,1,0:T(8,128)(2,1)S(1)}, u32[]{:S(2)}, u32[]{:S(2)}) collective-permute-start(bf16[2,72,896]{2,1,0:T(8,128)(2,1)S(1)} %pad_maximum_fusion.2.refs_4_), channel_id=1, source_target_pairs={{0,64},{1,65},{2,66},{3,67},{4,68},{5,69},{6,70},{7,71},{8,72},{9,... | collective-permute-start | bytes 774152 | tf_op jit(solution)/shard_map/cond/branch_0_fun/ppermute | solution.py:33
  24.2 5.8 %collective-permute-start.9 = (bf16[2,72,896]{2,1,0:T(8,128)(2,1)S(1)}, bf16[2,72,896]{2,1,0:T(8,128)(2,1)S(1)}, u32[]{:S(2)}, u32[]{:S(2)}) collective-permute-start(bf16[2,72,896]{2,1,0:T(8,128)(2,1)S(1)} %pad_maximum_fusion.2.refs_4_), channel_id=1, source_target_pairs={{0,192},{1,193},{2,194},{3,195},{4,196},{5,197},{6,198},{7,199},{8... | collective-permute-start | bytes 774152 | tf_op jit(solution)/shard_map/cond/branch_0_fun/ppermute | solution.py:33
  25.6 9.9 %collective-permute-start.10 = (bf16[2,72,896]{2,1,0:T(8,128)(2,1)S(1)}, bf16[2,72,896]{2,1,0:T(8,128)(2,1)S(1)}, u32[]{:S(2)}, u32[]{:S(2)}) collective-permute-start(bf16[2,72,896]{2,1,0:T(8,128)(2,1)S(1)} %pad_maximum_fusion.2.refs_4_), channel_id=1, source_target_pairs={{0,128},{1,129},{2,130},{3,131},{4,132},{5,133},{6,134},{7,135},{8... | collective-permute-start | bytes 774152 | tf_op jit(solution)/shard_map/cond/branch_0_fun/ppermute | solution.py:33
  27.3 8.4 %collective-permute-start.6 = (bf16[2,72,896]{2,1,0:T(8,128)(2,1)S(1)}, bf16[2,72,896]{2,1,0:T(8,128)(2,1)S(1)}, u32[]{:S(2)}, u32[]{:S(2)}) collective-permute-start(bf16[2,72,896]{2,1,0:T(8,128)(2,1)S(1)} %collective-permute-done.4.refs_3_), channel_id=1, source_target_pairs={{0,2},{1,3},{2,4},{3,5},{4,6},{5,7},{6,8},{7,9},{8,10},{9,11},{10,... | collective-permute-start | bytes 774152 | tf_op jit(solution)/shard_map/cond/branch_0_fun/ppermute | solution.py:33
  28.4 7.3 %collective-permute-start.7 = (bf16[2,72,896]{2,1,0:T(8,128)(2,1)S(1)}, bf16[2,72,896]{2,1,0:T(8,128)(2,1)S(1)}, u32[]{:S(2)}, u32[]{:S(2)}) collective-permute-start(bf16[2,72,896]{2,1,0:T(8,128)(2,1)S(1)} %collective-permute-done.5.down2), channel_id=1, source_target_pairs={{0,14},{1,15},{2,0},{3,1},{4,2},{5,3},{6,4},{7,5},{8,6},{9,7},{10,... | collective-permute-start | bytes 774152 | tf_op jit(solution)/shard_map/cond/branch_0_fun/ppermute | solution.py:33
  35.7 7.1 %collective-permute-start.11 = (bf16[8,72,896]{2,1,0:T(8,128)(2,1)S(1)}, bf16[8,72,896]{2,1,0:T(8,128)(2,1)S(1)}, u32[]{:S(2)}, u32[]{:S(2)}) collective-permute-start(bf16[8,72,896]{2,1,0:T(8,128)(2,1)S(1)} %pad_maximum_fusion), channel_id=1, source_target_pairs={{0,16},{1,17},{2,18},{3,19},{4,20},{5,21},{6,22},{7,23},{8,24},{9,... | collective-permute-start | bytes 3096584 | tf_op jit(solution)/shard_map/cond/branch_0_fun/ppermute | solution.py:33
  39.8 7.3 %collective-permute-start.12 = (bf16[1,72,896]{2,1,0:T(8,128)(2,1)S(1)}, bf16[1,72,896]{2,1,0:T(8,128)(2,1)S(1)}, u32[]{:S(2)}, u32[]{:S(2)}) collective-permute-start(bf16[1,72,896]{2,1,0:T(8,128)(2,1)S(1)} %slice.8), channel_id=1, source_target_pairs={{0,2},{1,3},{2,4},{3,5},{4,6},{5,7},{6,8},{7,9},{8,10},{9,11},{10,... | collective-permute-start | bytes 387080 | tf_op jit(solution)/shard_map/cond/branch_0_fun/ppermute | solution.py:33
  40.6 6.6 %copy-start = (f32[896,896]{1,0:T(8,128)S(1)}, f32[896,896]{1,0:T(8,128)}, u32[]{:S(2)}) copy-start(f32[896,896]{1,0:T(8,128)} %get-tuple-element.34.best_ref) | copy-start | bytes 9633796 | tf_op jit(solution)/shard_map/cond
  40.6 6.5 %collective-permute-start.13 = (bf16[1,72,896]{2,1,0:T(8,128)(2,1)S(1)}, bf16[1,72,896]{2,1,0:T(8,128)(2,1)S(1)}, u32[]{:S(2)}, u32[]{:S(2)}) collective-permute-start(bf16[1,72,896]{2,1,0:T(8,128)(2,1)S(1)} %slice.9), channel_id=1, source_target_pairs={{0,14},{1,15},{2,0},{3,1},{4,2},{5,3},{6,4},{7,5},{8,6},{9,7},{10,... | collective-permute-start | bytes 387080 | tf_op jit(solution)/shard_map/cond/branch_0_fun/ppermute | solution.py:33
  51.0 1.7 %copy-start.2 = (f32[896,896]{1,0:T(8,128)}, f32[896,896]{1,0:T(8,128)S(1)}, u32[]{:S(2)}) copy-start(f32[896,896]{1,0:T(8,128)S(1)} %get-tuple-element.143) | copy-start | bytes 9633796
